TPU v7x, 32 devices: a whole 2x2x4 slice. The times are simulated.
32 devices in a mesh: groups: 2 (over y), blk: 4 (over z), chan: 4 (over x, core).
Axes of the slice: x: 2, y: 2, z: 4, core: 2. Of those that a mesh axis runs over, the one named last changes fastest.
Arguments:
- fmap1: bfloat16 [128, 256, 128], P(('groups', 'blk'), 'chan'), parts along dimension 0, may hold values from -6 to 6
- fmap2: bfloat16 [128, 256, 128], P(('groups', 'blk'), 'chan'), parts along dimension 0, may hold values from -6 to 6
- windows: int32 [128, 20], P(('groups', 'blk')), parts along dimension 0, may hold values from 0 to 63, as said below
- live: int32 [128], P(('groups', 'blk')), parts along dimension 0, may hold values from 1 to 20, as said below
- cotangent: bfloat16 [128, 20, 128, 128], P(('groups', 'blk')), parts along dimension 0, may hold values from -6 to 6
Outputs:
- grad_one: float32 [128, 256, 128], P(('groups', 'blk'), 'chan'), parts along dimension 0
- grad_two: float32 [128, 256, 128], P(('groups', 'blk'), 'chan'), parts along dimension 0
There are 2 independent parts, one for each index of `groups`. A program takes and returns all parts, laid end to end along the dimension named above; each array names one. Nothing has to cross between parts.
Inputs may be any that keep to these rules, and one draw needn't show every extreme that they name: `windows`: the ids in one row are distinct; they may name blocks anywhere in the frame. Entries at slots live[b] and beyond are padding and carry no weight. `live`: some block uses all 20 slots.
All inputs are finite; a program needn't handle non-finite values.
Results may differ from a plain program's by a relative error of at most 0.0003.
Values may be sent and summed in bfloat16 or wider, within the bound.
A program may use at most 64 MiB of HBM per device.

v0:
```python
import math
import jax
import jax.numpy as jnp
from jax import lax
from jax.sharding import PartitionSpec as P

C = 256


def body(fmap1, fmap2, windows, live, cotangent):
    blocks, channels, site_count = fmap1.shape
    slot_count = windows.shape[1]
    inv_root = 1.0 / math.sqrt(C)
    slot_mask = (jnp.arange(slot_count, dtype=jnp.int32)[None, :] < live[:, None]).astype(
        jnp.float32
    )
    terms = jnp.einsum("bwij,bci->bwcj", cotangent, fmap1, preferred_element_type=jnp.float32)
    terms = terms * (inv_root * slot_mask)[:, :, None, None]
    flat_terms = terms.reshape(blocks * slot_count, channels * site_count)
    flat_ids = windows.reshape(-1)
    piece = lax.all_gather(fmap2, "blk", axis=0, tiled=True)
    piece_rows = piece.shape[0]
    row_ids = jnp.arange(piece_rows, dtype=jnp.int32)
    picker = (flat_ids[:, None] == row_ids[None, :]).astype(jnp.bfloat16)
    fetched = jnp.dot(
        picker, piece.reshape(piece_rows, channels * site_count), preferred_element_type=jnp.float32
    )
    fetched = fetched.astype(jnp.bfloat16).reshape(blocks, slot_count, channels, site_count)
    row_count = blocks * lax.axis_size("blk")
    row_ids = jnp.arange(row_count, dtype=jnp.int32)
    owner_hot = (row_ids[:, None] == flat_ids[None, :]).astype(jnp.float32)
    summed = jnp.dot(
        owner_hot, flat_terms, preferred_element_type=jnp.float32, precision=lax.Precision.HIGHEST
    )
    grad_two = lax.psum_scatter(
        summed.reshape(row_count, channels, site_count), "blk", scatter_dimension=0, tiled=True
    )
    selected = fetched * slot_mask.astype(jnp.bfloat16)[:, :, None, None]
    grad_one = (
        jnp.einsum("bwij,bwcj->bci", cotangent, selected, preferred_element_type=jnp.float32)
        * inv_root
    )
    return (grad_one, grad_two)


def solution(mesh):
    placed = (
        P(("groups", "blk"), "chan", None),
        P(("groups", "blk"), "chan", None),
        P(("groups", "blk"), None),
        P(("groups", "blk")),
        P(("groups", "blk"), None, None, None),
    )
    return jax.shard_map(
        body,
        mesh=mesh,
        in_specs=placed,
        out_specs=(P(("groups", "blk"), "chan", None), P(("groups", "blk"), "chan", None)),
        check_vma=False,
    )
```

profile of v0, /device:TPU:0, one launch (start us, length us, event | category | flops | bytes accessed | tf_op | source)
XLA Modules:
  0.0 94.8 jit_solution(12129404039623603795)
XLA Ops:
  7.2 0.0 copy-start
  7.2 0.0 all-gather.2.cloned.1.call-start
  7.2 0.7 all-gather.2.cloned.1.call-update
  7.9 0.0 reduce-scatter.2.cloned.1.call-start
  8.0 0.8 eq.28
  8.7 0.7 fusion.20
  9.5 0.0 copy-done
  9.5 4.9 %broadcast_multiply_fusion = f32[16,64,20,128]{3,1,2,0:T(8,128)S(1)} fusion(f32[16,20]{1,0:T(8,128)S(1)} %fusion.20, bf16[16,20,128,128]{3,2,1,0:T(8,128)(2,1)} %param.9, bf16[16,64,128]{2,1,0:T(8,128)(2,1)S(1)} %copy-done), kind=kOutput, calls=%fused_computation.5 | convolution fusion | flops 673710080 | bytes 21234944 | tf_op jit(solution)/shard_map/bwij,bci->bwcj/dot_general | solution.py:17
  14.4 0.0 copy-start.1
  14.4 11.9 %fusion = f32[64,64,128]{2,0,1:T(8,128)} fusion(s32[320]{0:T(512)S(1)} %eq.28, f32[40,8,64,128]{3,2,1,0:T(8,128)S(1)} %bitcast.38), kind=kOutput, calls=%fused_computation.2 | convolution fusion | flops 2013286400 | bytes 12584192 | tf_op jit(solution)/shard_map/dot_general | solution.py:32
  26.3 0.0 reduce-scatter.2.cloned.1.call-update
  26.3 0.0 copy-done.1
  26.3 0.1 convert_convert_fusion
  26.4 13.9 %all-gather.2.cloned.1.call-done = bf16[64,64,128]{2,1,0:T(8,128)(2,1)} async-done(((bf16[16,64,128]{2,1,0:T(8,128)(2,1)}), bf16[64,64,128]{2,1,0:T(8,128)(2,1)}) %all-gather.2.cloned.1.call-update) | async-done | bytes 1048592 | tf_op jit(solution)/shard_map/all_gather | solution.py:21
  40.2 2.8 %fusion.6 = bf16[40,8,64,128]{3,1,2,0:T(8,128)(2,1)S(1)} fusion(bf16[8,8,64,128]{3,2,1,0:T(8,128)(2,1)} %bitcast.40, s32[320]{0:T(512)S(1)} %eq.28), kind=kOutput, calls=%fused_computation.9 | convolution fusion | flops 338186240 | bytes 6292736 | tf_op jit(solution)/shard_map/dot_general | solution.py:25
  43.0 1.7 %copy.16 = bf16[40,8,64,128]{3,2,1,0:T(8,128)(2,1)S(1)} copy(bf16[40,8,64,128]{3,1,2,0:T(8,128)(2,1)S(1)} %fusion.6) | data formatting | bytes 10485760
  44.7 8.9 %fusion.10 = f32[16,64,128]{2,1,0:T(8,128)} fusion(bf16[16,20,128,128]{3,2,1,0:T(8,128)(2,1)} %param.9, bf16[16,20,64,128]{3,2,1,0:T(8,128)(2,1)S(1)} %bitcast.39, bf16[16,20]{1,0:T(8,128)(2,1)S(1)} %convert_convert_fusion), kind=kOutput, calls=%fused_computation.11 | convolution fusion | flops 673841152 | bytes 16253568 | tf_op jit(solution)/shard_map/bwij,bwcj->bci/dot_general | solution.py:40
  53.6 32.3 %reduce-scatter.2.cloned.1.call-done = f32[16,64,128]{2,0,1:T(8,128)} async-done(((f32[64,64,128]{2,0,1:T(8,128)}), f32[16,64,128]{2,0,1:T(8,128)}) %reduce-scatter.2.cloned.1.call-update) | async-done | bytes 524304 | tf_op jit(solution)/shard_map/reduce_scatter | solution.py:35
  85.9 2.0 %copy.11 = f32[16,64,128]{2,1,0:T(8,128)} copy(f32[16,64,128]{2,0,1:T(8,128)} %reduce-scatter.2.cloned.1.call-done) | data formatting | bytes 1048576
Async XLA Ops:
  7.2 2.3 %copy-start = (bf16[16,64,128]{2,1,0:T(8,128)(2,1)S(1)}, bf16[16,64,128]{2,1,0:T(8,128)(2,1)}, u32[]{:S(2)}) copy-start(bf16[16,64,128]{2,1,0:T(8,128)(2,1)} %param.5) | copy-start | bytes 786436
  7.2 33.1 %all-gather.2.cloned.1.call-start = ((), (), s32[]{:S(2)}) async-start(), calls=%async_computation.1 | async-start | bytes 1310720 | tf_op jit(solution)/shard_map/all_gather | solution.py:21
  7.9 78.0 %reduce-scatter.2.cloned.1.call-start = ((), (), s32[]{:S(2)}) async-start(), calls=%async_computation.2 | async-start | bytes 2621440 | tf_op jit(solution)/shard_map/reduce_scatter | solution.py:35
  14.4 11.9 %copy-start.1 = (s32[16]{0:T(128)S(1)}, s32[16]{0:T(128)}, u32[]{:S(2)}) copy-start(s32[16]{0:T(128)} %param.8) | copy-start | bytes 196
Sparse Core Ops, SparseCore 0:
  9.6 30.6 all-gather.1
  42.5 43.3 reduce-scatter.1
where the time goes:
time: 95 us; the launch traced here: 94.8 us
  waiting for transfers between devices  46.9 us (49%)
  matrix products  28.5 us (30%)
  between operations  14.1 us (15%)
  local copies, waits for them, and re-layouts  4.45 us (5%)
    reduce_scatter x1, waiting for transfers between devices, body(): lax.psum_scatter(summed.reshape(row_count, channels, site_count), 'blk',...  32.3 us
    all_gather x1, waiting for transfers between devices, body(): piece = lax.all_gather(fmap2, 'blk', axis=0, tiled=True)  13.9 us
    dot_general x1, matrix products, body(): jnp.dot(owner_hot, flat_terms, preferred_element_type=jnp.float32, precis...  11.9 us
    dot_general x1, matrix products, body(): jnp.einsum('bwij,bwcj->bci', cotangent, selected, preferred_element_type=...  8.92 us
    dot_general x1, matrix products, body(): jnp.einsum('bwij,bci->bwcj', cotangent, fmap1, preferred_element_type=jnp...  4.93 us
    unnamed x6, local copies, waits for them, and re-layouts  3.67 us
    dot_general x1, matrix products, body(): jnp.dot(picker, piece.reshape(piece_rows, channels * site_count), preferr...  2.79 us
  transfers between devices with their start and end apart: 2, of which 2 were waited for; matrix products, arithmetic and copies ran while one was open for 33% of the time, Pallas kernels for 0%

commit v1 on v0

--- a/solution.py
+++ b/solution.py
@@ -5,6 +5,30 @@
 from jax.sharding import PartitionSpec as P
 
 C = 256
+
+
+def _scan_circles(z_in, dim_i):
+    z_in = jnp.moveaxis(z_in, 0, dim_i)
+    side_arr = z_in.shape
+    extra = z_in.reshape(
+        *side_arr[:dim_i], side_arr[dim_i] * side_arr[dim_i + 1], *side_arr[dim_i + 2 :]
+    )
+    return extra
+
+
+def number_the_steps_all(patch, named_axis):
+    y2, current_arr = (lax.axis_size(named_axis), lax.axis_index(named_axis))
+    r_now, item_now = (patch[None], 1)
+    while item_now < y2:
+        x_now = lax.ppermute(
+            r_now, axis_name=named_axis, perm=tuple(((u, u ^ item_now) for u in range(y2)))
+        )
+        state_next = current_arr & item_now == 0
+        r_now = jnp.concatenate(
+            [jnp.where(state_next, r_now, x_now), jnp.where(state_next, x_now, r_now)]
+        )
+        item_now *= 2
+    return r_now
 
 
 def body(fmap1, fmap2, windows, live, cotangent):
@@ -18,7 +42,7 @@
     terms = terms * (inv_root * slot_mask)[:, :, None, None]
     flat_terms = terms.reshape(blocks * slot_count, channels * site_count)
     flat_ids = windows.reshape(-1)
-    piece = lax.all_gather(fmap2, "blk", axis=0, tiled=True)
+    piece = _scan_circles(number_the_steps_all(fmap2, "blk"), 0)
     piece_rows = piece.shape[0]
     row_ids = jnp.arange(piece_rows, dtype=jnp.int32)
     picker = (flat_ids[:, None] == row_ids[None, :]).astype(jnp.bfloat16)

time: 95 us -> 110 us (1.16)
  waiting for transfers between devices: 46.9 us -> 57 us
  starting transfers between devices: 0.08 us -> 5.93 us
  matrix products: 28.5 us -> 27.1 us
    ppermute x0 -> x2, waiting for transfers between devices: none -> 56.9 us  [number_the_steps_all(): lax.ppermute(r_now, axis_name=named_axis, perm=tuple(((u, u ^ item_now) f...]
    reduce_scatter x1, waiting for transfers between devices: 32.3 us -> 0.01 us  [body(): lax.psum_scatter(summed.reshape(row_count, channels, site_count), 'blk',...]
    all_gather x1 -> x0, waiting for transfers between devices: 13.9 us -> none  [body(): piece = lax.all_gather(fmap2, 'blk', axis=0, tiled=True)]
    ppermute x0 -> x2, starting transfers between devices: none -> 5.89 us  [number_the_steps_all(): lax.ppermute(r_now, axis_name=named_axis, perm=tuple(((u, u ^ item_now) f...]
    unnamed x6 -> x8, local copies, waits for them, and re-layouts: 3.67 us -> 3.51 us
  transfers between devices with their start and end apart: 2 -> 3, of which waited for: 2 -> 2; matrix products, arithmetic and copies ran while one was open for 33% -> 11% of each run, Pallas kernels for 0% -> 0%
where the time goes in v1:
time: 110 us
  waiting for transfers between devices  57 us (52%)
  matrix products  27.1 us (25%)
  between operations  14.1 us (13%)
  starting transfers between devices  5.93 us (5%)
  local copies, waits for them, and re-layouts  4.33 us (4%)
    ppermute x2, waiting for transfers between devices, number_the_steps_all(): lax.ppermute(r_now, axis_name=named_axis, perm=tuple(((u, u ^ item_now) f...  56.9 us
    dot_general x1, matrix products, body(): jnp.dot(owner_hot, flat_terms, preferred_element_type=jnp.float32, precis...  11.9 us
    dot_general x1, matrix products, body(): jnp.einsum('bwij,bwcj->bci', cotangent, selected, preferred_element_type=...  8.56 us
    ppermute x2, starting transfers between devices, number_the_steps_all(): lax.ppermute(r_now, axis_name=named_axis, perm=tuple(((u, u ^ item_now) f...  5.89 us
    dot_general x1, matrix products, body(): jnp.einsum('bwij,bci->bwcj', cotangent, fmap1, preferred_element_type=jnp...  4.94 us
    unnamed x8, local copies, waits for them, and re-layouts  3.51 us
  transfers between devices with their start and end apart: 3, of which 2 were waited for; matrix products, arithmetic and copies ran while one was open for 11% of the time, Pallas kernels for 0%

profile of v1, /device:TPU:0, one launch (start us, length us, event | category | flops | bytes accessed | tf_op | source)
XLA Modules:
  0.0 109.5 jit_solution(662155666734341930)
XLA Ops:
  7.2 0.0 copy-start
  7.2 0.0 reduce-scatter.2.cloned.1.call-start
  7.2 0.8 eq.34
  8.0 0.7 fusion.20
  8.8 0.0 copy-done
  8.8 4.9 %broadcast_multiply_fusion = f32[16,64,20,128]{3,1,2,0:T(8,128)S(1)} fusion(f32[16,20]{1,0:T(8,128)S(1)} %fusion.20, bf16[16,20,128,128]{3,2,1,0:T(8,128)(2,1)} %param.9, bf16[16,64,128]{2,1,0:T(8,128)(2,1)S(1)} %copy-done), kind=kOutput, calls=%fused_computation.5 | convolution fusion | flops 673710080 | bytes 21234944 | tf_op jit(solution)/shard_map/bwij,bci->bwcj/dot_general | solution.py:41
  13.7 0.0 copy-start.1
  13.7 0.0 copy-start.2
  13.7 11.9 %fusion = f32[64,64,128]{2,0,1:T(8,128)} fusion(s32[320]{0:T(512)S(1)} %eq.34, f32[40,8,64,128]{3,2,1,0:T(8,128)S(1)} %bitcast.42), kind=kOutput, calls=%fused_computation.2 | convolution fusion | flops 2013286400 | bytes 12584192 | tf_op jit(solution)/shard_map/dot_general | solution.py:56
  25.6 0.0 reduce-scatter.2.cloned.1.call-update
  25.6 0.0 copy-done.1
  25.6 3.1 %collective-permute-start = (bf16[1,16,64,128]{3,2,1,0:T(8,128)(2,1)S(1)}, bf16[1,16,64,128]{3,2,1,0:T(8,128)(2,1)S(1)}, u32[]{:S(2)}, u32[]{:S(2)}) collective-permute-start(bf16[1,16,64,128]{3,2,1,0:T(8,128)(2,1)S(1)} %bitcast.45), channel_id=1, source_target_pairs={{0,4},{4,0},{8,12},{12,8},{1,5},{5,1},{9,13},{13,9},{2,6},{6,2},{1... | collective-permute-start | bytes 786440 | tf_op jit(solution)/shard_map/ppermute | solution.py:23
  28.7 6.3 %collective-permute-done = bf16[1,16,64,128]{3,2,1,0:T(8,128)(2,1)S(1)} collective-permute-done((bf16[1,16,64,128]{3,2,1,0:T(8,128)(2,1)S(1)}, bf16[1,16,64,128]{3,2,1,0:T(8,128)(2,1)S(1)}, u32[]{:S(2)}, u32[]{:S(2)}) %collective-permute-start) | collective-permute-done | bytes 262176 | tf_op jit(solution)/shard_map/ppermute | solution.py:23
  35.1 0.1 pad_maximum_fusion.1
  35.1 2.8 %collective-permute-start.1 = (bf16[2,16,64,128]{3,2,1,0:T(8,128)(2,1)S(1)}, bf16[2,16,64,128]{3,2,1,0:T(8,128)(2,1)S(1)}, u32[]{:S(2)}, u32[]{:S(2)}) collective-permute-start(bf16[2,16,64,128]{3,2,1,0:T(8,128)(2,1)S(1)} %pad_maximum_fusion.1), channel_id=1, source_target_pairs={{0,8},{4,12},{8,0},{12,4},{1,9},{5,13},{9,1},{13,5},{2,10},{6,14},... | collective-permute-start | bytes 1572872 | tf_op jit(solution)/shard_map/ppermute | solution.py:23
  38.0 0.0 copy-done.2
  38.0 0.1 convert_convert_fusion
  38.0 50.6 %collective-permute-done.1 = bf16[2,16,64,128]{3,2,1,0:T(8,128)(2,1)S(1)} collective-permute-done((bf16[2,16,64,128]{3,2,1,0:T(8,128)(2,1)S(1)}, bf16[2,16,64,128]{3,2,1,0:T(8,128)(2,1)S(1)}, u32[]{:S(2)}, u32[]{:S(2)}) %collective-permute-start.1) | collective-permute-done | bytes 524320 | tf_op jit(solution)/shard_map/ppermute | solution.py:23
  88.6 0.1 broadcast_select_fusion.1
  88.7 0.1 pad_maximum_fusion
  88.8 1.8 %fusion.6 = bf16[40,8,64,128]{3,1,2,0:T(8,128)(2,1)S(1)} fusion(bf16[8,8,64,128]{3,2,1,0:T(8,128)(2,1)S(1)} %bitcast.44, s32[320]{0:T(512)S(1)} %eq.34), kind=kOutput, calls=%fused_computation.9 | convolution fusion | flops 338186240 | bytes 6292736 | tf_op jit(solution)/shard_map/dot_general | solution.py:49
  90.6 1.5 %copy.14 = bf16[40,8,64,128]{3,2,1,0:T(8,128)(2,1)S(1)} copy(bf16[40,8,64,128]{3,1,2,0:T(8,128)(2,1)S(1)} %fusion.6) | data formatting | bytes 10485760
  92.1 8.6 %fusion.10 = f32[16,64,128]{2,1,0:T(8,128)} fusion(bf16[16,20,128,128]{3,2,1,0:T(8,128)(2,1)} %param.9, bf16[16,20,64,128]{3,2,1,0:T(8,128)(2,1)S(1)} %bitcast.43, bf16[16,20]{1,0:T(8,128)(2,1)S(1)} %convert_convert_fusion), kind=kOutput, calls=%fused_computation.11 | convolution fusion | flops 673841152 | bytes 16253568 | tf_op jit(solution)/shard_map/bwij,bwcj->bci/dot_general | solution.py:64
  100.7 0.0 reduce-scatter.2.cloned.1.call-done
  100.7 2.0 %copy.9 = f32[16,64,128]{2,1,0:T(8,128)} copy(f32[16,64,128]{2,0,1:T(8,128)} %reduce-scatter.2.cloned.1.call-done) | data formatting | bytes 1048576
  (1 shorter events, 0.0 us)
Async XLA Ops:
  7.2 1.6 %copy-start = (bf16[16,64,128]{2,1,0:T(8,128)(2,1)S(1)}, bf16[16,64,128]{2,1,0:T(8,128)(2,1)}, u32[]{:S(2)}) copy-start(bf16[16,64,128]{2,1,0:T(8,128)(2,1)} %param.5) | copy-start | bytes 786436
  7.2 93.5 %reduce-scatter.2.cloned.1.call-start = ((), (), s32[]{:S(2)}) async-start(), calls=%async_computation.1 | async-start | bytes 2621440 | tf_op jit(solution)/shard_map/reduce_scatter | solution.py:59
  13.7 11.9 %copy-start.1 = (bf16[16,64,128]{2,1,0:T(8,128)(2,1)S(1)}, bf16[16,64,128]{2,1,0:T(8,128)(2,1)}, u32[]{:S(2)}) copy-start(bf16[16,64,128]{2,1,0:T(8,128)(2,1)} %param.6) | copy-start | bytes 786436
  13.7 24.2 %copy-start.2 = (s32[16]{0:T(128)S(1)}, s32[16]{0:T(128)}, u32[]{:S(2)}) copy-start(s32[16]{0:T(128)} %param.8) | copy-start | bytes 196
  25.6 9.4 %collective-permute-start = (bf16[1,16,64,128]{3,2,1,0:T(8,128)(2,1)S(1)}, bf16[1,16,64,128]{3,2,1,0:T(8,128)(2,1)S(1)}, u32[]{:S(2)}, u32[]{:S(2)}) collective-permute-start(bf16[1,16,64,128]{3,2,1,0:T(8,128)(2,1)S(1)} %bitcast.45), channel_id=1, source_target_pairs={{0,4},{4,0},{8,12},{12,8},{1,5},{5,1},{9,13},{13,9},{2,6},{6,2},{1... | collective-permute-start | bytes 786440 | tf_op jit(solution)/shard_map/ppermute | solution.py:23
  35.1 53.5 %collective-permute-start.1 = (bf16[2,16,64,128]{3,2,1,0:T(8,128)(2,1)S(1)}, bf16[2,16,64,128]{3,2,1,0:T(8,128)(2,1)S(1)}, u32[]{:S(2)}, u32[]{:S(2)}) collective-permute-start(bf16[2,16,64,128]{3,2,1,0:T(8,128)(2,1)S(1)} %pad_maximum_fusion.1), channel_id=1, source_target_pairs={{0,8},{4,12},{8,0},{12,4},{1,9},{5,13},{9,1},{13,5},{2,10},{6,14},... | collective-permute-start | bytes 1572872 | tf_op jit(solution)/shard_map/ppermute | solution.py:23
Sparse Core Ops, SparseCore 0:
  25.7 66.2 reduce-scatter.1
